TPU v7x, 32 devices: a whole 2x2x4 slice. The times are simulated.
32 devices in a mesh: dp: 8 (over z, x), mp: 4 (over y, core).
Axes of the slice: x: 2, y: 2, z: 4, core: 2. Of those that a mesh axis runs over, the one named last changes fastest.
Arguments:
- block_input: bfloat16 [2048, 1152], P(('dp', 'mp')), may hold values from -6 to 6
- segments: int32 [8, 512], P('dp'), may hold values from 0 to 4, as said below
- attend_gain: bfloat16 [2, 576], replicated, may hold values from 0.5 to 1.5
- query_weight: bfloat16 [2, 576, 576], P(None, 'dp', 'mp'), may hold values from -0.25 to 0.25
- key_weight: bfloat16 [2, 576, 192], P(None, 'dp', 'mp'), may hold values from -0.25 to 0.25
- value_weight: bfloat16 [2, 576, 192], P(None, 'dp', 'mp'), may hold values from -0.25 to 0.25
- mix_weight: bfloat16 [2, 576, 576], P(None, 'mp', 'dp'), may hold values from -1 to 1
- feed_gain: bfloat16 [2, 576], replicated, may hold values from 0.5 to 1.5
- gate_weight: bfloat16 [2, 576, 1536], P(None, 'dp', 'mp'), may hold values from -0.25 to 0.25
- up_weight: bfloat16 [2, 576, 1536], P(None, 'dp', 'mp'), may hold values from -0.25 to 0.25
- down_weight: bfloat16 [2, 1536, 576], P(None, 'mp', 'dp'), may hold values from -0.3125 to 0.3125
- cotangent: bfloat16 [2048, 1152], P(('dp', 'mp')), may hold values from -6 to 6
Outputs:
- block_output: bfloat16 [2048, 1152], P(('dp', 'mp'))
- input_grad: float32 [2048, 1152], P(('dp', 'mp'))
- attend_gain_grad: float32 [2, 576], replicated
- query_grad: float32 [2, 576, 576], P(None, 'dp', 'mp')
- key_grad: float32 [2, 576, 192], P(None, 'dp', 'mp')
- value_grad: float32 [2, 576, 192], P(None, 'dp', 'mp')
- mix_grad: float32 [2, 576, 576], P(None, 'mp', 'dp')
- feed_gain_grad: float32 [2, 576], replicated
- gate_grad: float32 [2, 576, 1536], P(None, 'dp', 'mp')
- up_grad: float32 [2, 576, 1536], P(None, 'dp', 'mp')
- down_grad: float32 [2, 1536, 576], P(None, 'mp', 'dp')
Inputs may be any that keep to these rules, and one draw needn't show every extreme that they name: `segments`: segment numbers never fall along a sequence and may skip values; in every sequence one segment holds both position 127 and position 384.
All inputs are finite; a program needn't handle non-finite values.
Results may differ from a plain program's by a relative error of at most 0.034.
Values may be sent and summed in bfloat16 or wider, within the bound.
A program may use at most 128 MiB of HBM per device.

v0:
```python
import math

import jax
import jax.numpy as jnp
from jax import lax
from jax.sharding import PartitionSpec as P

HEADS = 9
KV_HEADS = 3
HEAD_DIM = 64
LAYERS = 2


norm_eps = 1e-05
rope_base = 100000.0
masked_value = -1e30


def in_blocks(shard, dim, peers):
    dims = shard.shape
    pieces = shard.reshape(*dims[:dim], peers, dims[dim] // peers, *dims[dim + 1 :])
    return jnp.moveaxis(pieces, dim, 0)


def sent_and_summed(shard, axis, dim):
    peers = lax.axis_size(axis)
    pieces = lax.all_to_all(in_blocks(shard, dim, peers), axis, 0, 0, tiled=True)
    return jnp.sum(pieces.astype(jnp.float32), axis=0)


def side_by_side(arrays, axis, dim, along):
    ends, at = ([], 0)
    for a in arrays[:-1]:
        at += a.shape[along]
        ends.append(at)
    both = jnp.concatenate(arrays, axis=along)
    return tuple(jnp.split(sent_and_summed(both, axis, dim), ends, axis=along))


def doc_positions(seg_ids):
    length_all = seg_ids.shape[-1]
    token_index = jnp.arange(length_all, dtype=jnp.int32)
    starts = jnp.concatenate(
        [token_index[..., :1] == 0, seg_ids[..., 1:] != seg_ids[..., :-1]], axis=-1
    )
    doc_start = lax.cummax(jnp.where(starts, token_index, 0), axis=seg_ids.ndim - 1)
    return token_index - doc_start


def rope_tables(positions):
    half_dim = HEAD_DIM // 2
    exponents = jnp.arange(half_dim, dtype=jnp.float32) * (2.0 / HEAD_DIM)
    inverse = jnp.exp(-math.log(rope_base) * exponents)
    angles = positions.astype(jnp.float32)[..., None] * inverse
    cosine = jnp.cos(angles)
    sine = jnp.sin(angles)
    return (jnp.concatenate([cosine, cosine], axis=-1), jnp.concatenate([sine, sine], axis=-1))


def rotate(values, cosine, sine):
    half_dim = values.shape[-1] // 2
    turned = jnp.concatenate([-values[..., half_dim:], values[..., :half_dim]], axis=-1)
    return values * cosine[..., None, :] + turned * sine[..., None, :]


def matmul_f32(left, right):
    return jnp.dot(left, right, preferred_element_type=jnp.float32)


def inner_rows(left, right):
    return lax.dot_general(
        left, right, (((0,), (0,)), ((), ())), preferred_element_type=jnp.float32
    )


def inner_cols(left, right):
    return lax.dot_general(
        left, right, (((1,), (1,)), ((), ())), preferred_element_type=jnp.float32
    )


def norm_in(residual, gain):
    rows_f32 = residual.astype(jnp.bfloat16).astype(jnp.float32)
    row_scale = lax.rsqrt(jnp.mean(rows_f32 * rows_f32, axis=1, keepdims=True) + norm_eps)
    normed = (rows_f32 * row_scale * gain.astype(jnp.float32)).astype(jnp.bfloat16)
    normed_all = lax.all_gather(normed, "mp", axis=0, tiled=True)
    return (rows_f32, row_scale, normed_all)


def attend_gather(query_part, key_part, value_part, mix_part):
    return (
        lax.all_gather(query_part, "dp", axis=0, tiled=True),
        lax.all_gather(key_part, "dp", axis=0, tiled=True),
        lax.all_gather(value_part, "dp", axis=0, tiled=True),
        lax.all_gather(mix_part, "dp", axis=1, tiled=True),
    )


def feed_gather(gate_part, up_part, down_part):
    return (
        lax.all_gather(gate_part, "dp", axis=0, tiled=True),
        lax.all_gather(up_part, "dp", axis=0, tiled=True),
        lax.all_gather(down_part, "dp", axis=1, tiled=True),
    )


def share_sum(partial_value):
    return lax.psum_scatter(
        partial_value.astype(jnp.bfloat16), "mp", scatter_dimension=0, tiled=True
    ).astype(jnp.float32)


def to_rows(packed):
    return lax.all_to_all(packed, "mp", split_axis=0, concat_axis=1, tiled=True)


def to_cols(packed):
    return lax.all_to_all(packed, "mp", split_axis=1, concat_axis=0, tiled=True)


def spread_grad(gradient):
    return lax.all_gather(gradient.astype(jnp.bfloat16), "mp", axis=0, tiled=True)


def norm_back(grad_normed, rows_f32, row_scale, gain):
    width = rows_f32.shape[1]
    gain_f32 = gain.astype(jnp.float32)
    cubed = row_scale * row_scale * row_scale
    inner = jnp.sum(grad_normed * gain_f32 * rows_f32, axis=1, keepdims=True)
    resid_grad = gain_f32 * row_scale * grad_normed - rows_f32 * cubed * inner / width
    gain_term = jnp.sum(grad_normed * rows_f32 * row_scale, axis=0)
    return (resid_grad, gain_term)


def head_views(query_turned, keys_all, values_all):
    own_rows = query_turned.shape[0]
    group_size = HEADS // KV_HEADS
    query_heads = query_turned.reshape(own_rows, KV_HEADS, group_size, HEAD_DIM)
    key_heads = keys_all.reshape(keys_all.shape[0], KV_HEADS, HEAD_DIM)
    value_heads = values_all.reshape(values_all.shape[0], KV_HEADS, HEAD_DIM)
    return (query_heads, key_heads, value_heads)


def masked_logits(query_heads, key_heads, allowed):
    scores = jnp.einsum(
        "qkgd,tkd->kgqt", query_heads, key_heads, preferred_element_type=jnp.float32
    )
    return jnp.where(allowed, scores * (1.0 / math.sqrt(HEAD_DIM)), masked_value)


def attend(query_turned, keys_all, values_all, allowed):
    query_heads, key_heads, value_heads = head_views(query_turned, keys_all, values_all)
    logits = masked_logits(query_heads, key_heads, allowed)
    row_max = jnp.max(logits, axis=3, keepdims=True)
    raised = jnp.exp(logits - row_max)
    row_total = jnp.sum(raised, axis=3, keepdims=True)
    weights_low = (raised / row_total).astype(jnp.bfloat16)
    mixed = jnp.einsum(
        "kgqt,tkd->qkgd", weights_low, value_heads, preferred_element_type=jnp.float32
    )
    return (mixed.reshape(query_turned.shape[0], -1), row_max + jnp.log(row_total))


def attend_back(query_turned, keys_all, values_all, allowed, log_total, grad_mixed):
    query_heads, key_heads, value_heads = head_views(query_turned, keys_all, values_all)
    logits = masked_logits(query_heads, key_heads, allowed)
    weights = jnp.exp(logits - log_total)
    grad_heads = grad_mixed.reshape(query_heads.shape)
    grad_weights = jnp.einsum(
        "qkgd,tkd->kgqt", grad_heads, value_heads, preferred_element_type=jnp.float32
    )
    delta = jnp.sum(weights * grad_weights, axis=3, keepdims=True)
    grad_scores = (weights * (grad_weights - delta) * (1.0 / math.sqrt(HEAD_DIM))).astype(
        jnp.bfloat16
    )
    grad_query = jnp.einsum(
        "kgqt,tkd->qkgd", grad_scores, key_heads, preferred_element_type=jnp.float32
    )
    grad_keys = jnp.einsum(
        "kgqt,qkgd->tkd", grad_scores, query_heads, preferred_element_type=jnp.float32
    )
    grad_values = jnp.einsum(
        "kgqt,qkgd->tkd",
        weights.astype(jnp.bfloat16),
        grad_heads,
        preferred_element_type=jnp.float32,
    )
    row_count = keys_all.shape[0]
    return (
        grad_query.reshape(query_turned.shape[0], -1),
        grad_keys.reshape(row_count, -1),
        grad_values.reshape(row_count, -1),
    )


def on_device(
    block_input,
    segments,
    attend_gain,
    query_weight,
    key_weight,
    value_weight,
    mix_weight,
    feed_gain,
    gate_weight,
    up_weight,
    down_weight,
    cotangent,
):
    width = block_input.shape[1] // 2
    own_rows = block_input.shape[0] * 2
    model_parts = lax.axis_size("mp")
    row_count = own_rows * model_parts
    my_index = lax.axis_index("mp")
    first_row = my_index * own_rows
    seg_ids = segments[0]
    positions = doc_positions(seg_ids)
    my_segs = lax.dynamic_slice_in_dim(seg_ids, first_row, own_rows, 0)
    cosine, sine = rope_tables(lax.dynamic_slice_in_dim(positions, first_row, own_rows, 0))
    key_index = jnp.arange(row_count, dtype=jnp.int32)
    query_index = first_row + jnp.arange(own_rows, dtype=jnp.int32)
    allowed = (key_index[None, :] <= query_index[:, None]) & (seg_ids[None, :] == my_segs[:, None])
    query_width = query_weight.shape[2]
    kv_width = key_weight.shape[2]
    residual = block_input.reshape(own_rows, width).astype(jnp.float32)
    attend_saved = []
    feed_saved = []
    for layer_index in range(LAYERS):
        rows_f32, row_scale, normed = norm_in(residual, attend_gain[layer_index])
        attend_full = attend_gather(
            query_weight[layer_index],
            key_weight[layer_index],
            value_weight[layer_index],
            mix_weight[layer_index],
        )
        packed = jnp.concatenate(
            [
                matmul_f32(normed, attend_full[0]),
                matmul_f32(normed, attend_full[1]),
                matmul_f32(normed, attend_full[2]),
            ],
            axis=1,
        ).astype(jnp.bfloat16)
        row_view = to_rows(packed).reshape(own_rows, model_parts, -1)
        query_rows = (
            row_view[:, :, :query_width].reshape(own_rows, HEADS, HEAD_DIM).astype(jnp.float32)
        )
        key_rows = (
            row_view[:, :, query_width : query_width + kv_width]
            .reshape(own_rows, KV_HEADS, HEAD_DIM)
            .astype(jnp.float32)
        )
        value_rows = row_view[:, :, query_width + kv_width :].reshape(own_rows, -1)
        query_turned = rotate(query_rows, cosine, sine).reshape(own_rows, -1).astype(jnp.bfloat16)
        key_turned = rotate(key_rows, cosine, sine).reshape(own_rows, -1).astype(jnp.bfloat16)
        keys_all, values_all = (
            lax.all_gather(key_turned, "mp", axis=0, tiled=True),
            lax.all_gather(value_rows, "mp", axis=0, tiled=True),
        )
        mixed, log_total = attend(query_turned, keys_all, values_all, allowed)
        mixed_block = to_cols(mixed.astype(jnp.bfloat16))
        residual = residual + share_sum(matmul_f32(mixed_block, attend_full[3]))
        attend_saved.append(
            (
                rows_f32,
                row_scale,
                normed,
                query_turned,
                keys_all,
                values_all,
                log_total,
                mixed_block,
                attend_full,
            )
        )
        rows_two, scale_two, normed_two = norm_in(residual, feed_gain[layer_index])
        feed_full = feed_gather(
            gate_weight[layer_index], up_weight[layer_index], down_weight[layer_index]
        )
        gate_out = matmul_f32(normed_two, feed_full[0])
        up_out = matmul_f32(normed_two, feed_full[1])
        hidden = (jax.nn.silu(gate_out) * up_out).astype(jnp.bfloat16)
        residual = residual + share_sum(matmul_f32(hidden, feed_full[2]))
        feed_saved.append((rows_two, scale_two, normed_two, gate_out, up_out, hidden, feed_full))
    block_output = residual.astype(jnp.bfloat16).reshape(own_rows // 2, 2 * width)
    grad_resid = cotangent.reshape(own_rows, width).astype(jnp.float32)
    attend_terms = [None] * LAYERS
    feed_terms = [None] * LAYERS
    query_grads = [None] * LAYERS
    key_grads = [None] * LAYERS
    value_grads = [None] * LAYERS
    mix_grads = [None] * LAYERS
    gate_grads = [None] * LAYERS
    up_grads = [None] * LAYERS
    down_grads = [None] * LAYERS
    for layer_index in range(LAYERS - 1, -1, -1):
        rows_two, scale_two, normed_two, gate_out, up_out, hidden, feed_full = feed_saved[
            layer_index
        ]
        gate_full, up_full, down_full = feed_gather(
            gate_weight[layer_index], up_weight[layer_index], down_weight[layer_index]
        )
        grad_full = spread_grad(grad_resid)
        grad_hidden = inner_cols(grad_full, down_full)
        down_term = inner_rows(hidden, grad_full)
        sigmoid_gate = jax.nn.sigmoid(gate_out)
        grad_gate = (
            grad_hidden * up_out * sigmoid_gate * (1.0 + gate_out * (1.0 - sigmoid_gate))
        ).astype(jnp.bfloat16)
        grad_up = (grad_hidden * gate_out * sigmoid_gate).astype(jnp.bfloat16)
        gate_term = inner_rows(normed_two, grad_gate)
        up_term = inner_rows(normed_two, grad_up)
        grad_normed = share_sum(inner_cols(grad_gate, gate_full) + inner_cols(grad_up, up_full))
        resid_grad, feed_terms[layer_index] = norm_back(
            grad_normed, rows_two, scale_two, feed_gain[layer_index]
        )
        grad_resid = grad_resid + resid_grad
        gate_grads[layer_index], up_grads[layer_index], down_grads[layer_index] = (
            *side_by_side(
                (gate_term.astype(jnp.bfloat16), up_term.astype(jnp.bfloat16)), "dp", 0, 1
            ),
            sent_and_summed(down_term.astype(jnp.bfloat16), "dp", 1),
        )
        (
            rows_f32,
            row_scale,
            normed,
            query_turned,
            keys_all,
            values_all,
            log_total,
            mixed_block,
            attend_full,
        ) = attend_saved[layer_index]
        query_full, key_full, value_full, mix_full = attend_gather(
            query_weight[layer_index],
            key_weight[layer_index],
            value_weight[layer_index],
            mix_weight[layer_index],
        )
        grad_full = spread_grad(grad_resid)
        grad_block = inner_cols(grad_full, mix_full).astype(jnp.bfloat16)
        mix_term = inner_rows(mixed_block, grad_full)
        grad_mixed = to_rows(grad_block)
        grad_query, grad_keys, grad_values = attend_back(
            query_turned, keys_all, values_all, allowed, log_total, grad_mixed
        )
        keys_own, values_own = (
            lax.psum_scatter(
                grad_keys.astype(jnp.bfloat16), "mp", scatter_dimension=0, tiled=True
            ).astype(jnp.float32),
            lax.psum_scatter(
                grad_values.astype(jnp.bfloat16), "mp", scatter_dimension=0, tiled=True
            ).astype(jnp.float32),
        )
        query_back = rotate(grad_query.reshape(own_rows, HEADS, HEAD_DIM), cosine, -sine).reshape(
            own_rows, model_parts, -1
        )
        key_back = rotate(keys_own.reshape(own_rows, KV_HEADS, HEAD_DIM), cosine, -sine).reshape(
            own_rows, model_parts, -1
        )
        value_back = values_own.reshape(own_rows, model_parts, -1)
        packed_grad = (
            jnp.concatenate([query_back, key_back, value_back], axis=2)
            .reshape(own_rows, -1)
            .astype(jnp.bfloat16)
        )
        column_grad = to_cols(packed_grad)
        grad_qcols = column_grad[:, :query_width]
        grad_kcols = column_grad[:, query_width : query_width + kv_width]
        grad_vcols = column_grad[:, query_width + kv_width :]
        query_term = inner_rows(normed, grad_qcols)
        key_term = inner_rows(normed, grad_kcols)
        value_term = inner_rows(normed, grad_vcols)
        grad_normed = share_sum(
            inner_cols(grad_qcols, query_full)
            + inner_cols(grad_kcols, key_full)
            + inner_cols(grad_vcols, value_full)
        )
        resid_grad, attend_terms[layer_index] = norm_back(
            grad_normed, rows_f32, row_scale, attend_gain[layer_index]
        )
        grad_resid = grad_resid + resid_grad
        (
            query_grads[layer_index],
            key_grads[layer_index],
            value_grads[layer_index],
            mix_grads[layer_index],
        ) = (
            *side_by_side(
                (
                    query_term.astype(jnp.bfloat16),
                    key_term.astype(jnp.bfloat16),
                    value_term.astype(jnp.bfloat16),
                ),
                "dp",
                0,
                1,
            ),
            sent_and_summed(mix_term.astype(jnp.bfloat16), "dp", 1),
        )
    attend_total, feed_total = lax.psum(
        (jnp.stack(attend_terms), jnp.stack(feed_terms)), ("dp", "mp")
    )
    input_grad = grad_resid.reshape(own_rows // 2, 2 * width)
    return (
        block_output,
        input_grad,
        attend_total,
        jnp.stack(query_grads),
        jnp.stack(key_grads),
        jnp.stack(value_grads),
        jnp.stack(mix_grads),
        feed_total,
        jnp.stack(gate_grads),
        jnp.stack(up_grads),
        jnp.stack(down_grads),
    )


def solution(mesh):
    in_specs = (
        P(("dp", "mp"), None),
        P("dp", None),
        P(),
        P(None, "dp", "mp"),
        P(None, "dp", "mp"),
        P(None, "dp", "mp"),
        P(None, "mp", "dp"),
        P(),
        P(None, "dp", "mp"),
        P(None, "dp", "mp"),
        P(None, "mp", "dp"),
        P(("dp", "mp"), None),
    )
    out_specs = (
        P(("dp", "mp"), None),
        P(("dp", "mp"), None),
        P(),
        P(None, "dp", "mp"),
        P(None, "dp", "mp"),
        P(None, "dp", "mp"),
        P(None, "mp", "dp"),
        P(),
        P(None, "dp", "mp"),
        P(None, "dp", "mp"),
        P(None, "mp", "dp"),
    )
    return jax.shard_map(
        on_device, mesh=mesh, in_specs=in_specs, out_specs=out_specs, check_vma=False
    )
```

profile of v0, /device:TPU:11, one launch (start us, length us, event | category | flops | bytes accessed | tf_op | source)
XLA Modules:
  0.0 1039.0 jit_solution(14695290921002256616)
XLA Ops:
  11.1 22.1 %all-gather.1 = bf16[1,576,48]{2,0,1:T(2,128)(2,1)S(1)} all-gather(bf16[1,72,48]{2,0,1:T(2,128)(2,1)S(1)} %copy.226), channel_id=3, replica_groups=mesh['dp'=8,'mp'=4] {'dp'}, dimensions={1}, use_global_device_ids=true | all-gather | bytes 62208 | tf_op jit(solution)/shard_map/all_gather | solution.py:93
  33.3 24.8 %all-gather.2 = bf16[1,576,48]{2,0,1:T(2,128)(2,1)S(1)} all-gather(bf16[1,72,48]{2,0,1:T(2,128)(2,1)S(1)} %copy.227), channel_id=4, replica_groups=mesh['dp'=8,'mp'=4] {'dp'}, dimensions={1}, use_global_device_ids=true | all-gather | bytes 62208 | tf_op jit(solution)/shard_map/all_gather | solution.py:94
  58.3 24.9 %all-gather = bf16[1,576,144]{2,1,0:T(8,128)(2,1)S(1)} all-gather(bf16[1,72,144]{2,1,0:T(8,128)(2,1)S(1)} %get-tuple-element.130), channel_id=2, replica_groups=mesh['dp'=8,'mp'=4] {'dp'}, dimensions={1}, use_global_device_ids=true | all-gather | bytes 186624 | tf_op jit(solution)/shard_map/all_gather | solution.py:92
  85.2 27.0 %all_gather.92 = bf16[512,576]{1,0:T(8,128)(2,1)S(1)} all-gather(bf16[128,576]{1,0:T(8,128)(2,1)S(1)} %multiply_convert_fusion.6), channel_id=1, replica_groups=mesh['dp'=8,'mp'=4] {'mp'}, dimensions={0}, use_global_device_ids=true | all-gather | bytes 737280 | tf_op jit(solution)/shard_map/all_gather | solution.py:86
  140.7 25.3 %all-gather.3 = bf16[1,144,576]{1,0,2:T(2,128)(2,1)S(1)} all-gather(bf16[1,144,72]{1,0,2:T(2,128)(2,1)S(1)} %copy.228), channel_id=5, replica_groups=mesh['dp'=8,'mp'=4] {'dp'}, dimensions={2}, use_global_device_ids=true | all-gather | bytes 186624 | tf_op jit(solution)/shard_map/all_gather | solution.py:95
  169.1 24.6 %all-gather.6 = bf16[1,384,576]{1,2,0:T(8,128)(2,1)S(1)} all-gather(bf16[1,384,72]{1,2,0:T(8,128)(2,1)S(1)} %get-tuple-element.112), channel_id=8, replica_groups=mesh['dp'=8,'mp'=4] {'dp'}, dimensions={2}, use_global_device_ids=true | all-gather | bytes 497664 | tf_op jit(solution)/shard_map/all_gather | solution.py:103
  194.4 25.9 %all-gather.5 = bf16[1,576,384]{2,1,0:T(8,128)(2,1)S(1)} all-gather(bf16[1,72,384]{2,1,0:T(8,128)(2,1)S(1)} %get-tuple-element.116), channel_id=7, replica_groups=mesh['dp'=8,'mp'=4] {'dp'}, dimensions={1}, use_global_device_ids=true | all-gather | bytes 497664 | tf_op jit(solution)/shard_map/all_gather | solution.py:102
  221.0 24.8 %all-gather.4 = bf16[1,576,384]{2,1,0:T(8,128)(2,1)S(1)} all-gather(bf16[1,72,384]{2,1,0:T(8,128)(2,1)S(1)} %get-tuple-element.114), channel_id=6, replica_groups=mesh['dp'=8,'mp'=4] {'dp'}, dimensions={1}, use_global_device_ids=true | all-gather | bytes 497664 | tf_op jit(solution)/shard_map/all_gather | solution.py:101
  247.7 32.8 %all_gather.99 = bf16[512,576]{1,0:T(8,128)(2,1)S(1)} all-gather(bf16[128,576]{1,0:T(8,128)(2,1)S(1)} %fusion.82), channel_id=1, replica_groups=mesh['dp'=8,'mp'=4] {'mp'}, dimensions={0}, use_global_device_ids=true | all-gather | bytes 737280 | tf_op jit(solution)/shard_map/all_gather | solution.py:86
  285.2 24.9 %all-gather.9 = bf16[1,576,48]{2,0,1:T(2,128)(2,1)S(1)} all-gather(bf16[1,72,48]{2,0,1:T(2,128)(2,1)S(1)} %copy.230), channel_id=11, replica_groups=mesh['dp'=8,'mp'=4] {'dp'}, dimensions={1}, use_global_device_ids=true | all-gather | bytes 62208 | tf_op jit(solution)/shard_map/all_gather | solution.py:94
  310.3 24.7 %all-gather.8 = bf16[1,576,48]{2,0,1:T(2,128)(2,1)S(1)} all-gather(bf16[1,72,48]{2,0,1:T(2,128)(2,1)S(1)} %copy.229), channel_id=10, replica_groups=mesh['dp'=8,'mp'=4] {'dp'}, dimensions={1}, use_global_device_ids=true | all-gather | bytes 62208 | tf_op jit(solution)/shard_map/all_gather | solution.py:93
  335.1 24.5 %all-gather.7 = bf16[1,576,144]{2,1,0:T(8,128)(2,1)S(1)} all-gather(bf16[1,72,144]{2,1,0:T(8,128)(2,1)S(1)} %copy-done.74), channel_id=9, replica_groups=mesh['dp'=8,'mp'=4] {'dp'}, dimensions={1}, use_global_device_ids=true | all-gather | bytes 186624 | tf_op jit(solution)/shard_map/all_gather | solution.py:92
  361.5 25.2 %all_gather.103 = bf16[512,576]{1,0:T(8,128)(2,1)S(1)} all-gather(bf16[128,576]{1,0:T(8,128)(2,1)S(1)} %fusion.90), channel_id=1, replica_groups=mesh['dp'=8,'mp'=4] {'mp'}, dimensions={0}, use_global_device_ids=true | all-gather | bytes 737280 | tf_op jit(solution)/shard_map/all_gather | solution.py:86
  413.9 25.8 %all-gather.10 = bf16[1,144,576]{1,0,2:T(2,128)(2,1)S(1)} all-gather(bf16[1,144,72]{1,0,2:T(2,128)(2,1)S(1)} %copy.231), channel_id=12, replica_groups=mesh['dp'=8,'mp'=4] {'dp'}, dimensions={2}, use_global_device_ids=true | all-gather | bytes 186624 | tf_op jit(solution)/shard_map/all_gather | solution.py:95
  442.3 26.9 %all-gather.13 = bf16[1,384,576]{1,2,0:T(8,128)(2,1)} all-gather(bf16[1,384,72]{1,2,0:T(8,128)(2,1)S(1)} %copy-done.72), channel_id=15, replica_groups=mesh['dp'=8,'mp'=4] {'dp'}, dimensions={2}, use_global_device_ids=true | all-gather | bytes 497664 | tf_op jit(solution)/shard_map/all_gather | solution.py:103
  469.2 26.6 %all-gather.12 = bf16[1,576,384]{2,1,0:T(8,128)(2,1)S(1)} all-gather(bf16[1,72,384]{2,1,0:T(8,128)(2,1)} %get-tuple-element.115), channel_id=14, replica_groups=mesh['dp'=8,'mp'=4] {'dp'}, dimensions={1}, use_global_device_ids=true | all-gather | bytes 497664 | tf_op jit(solution)/shard_map/all_gather | solution.py:102
  495.8 26.5 %all-gather.11 = bf16[1,576,384]{2,1,0:T(8,128)(2,1)} all-gather(bf16[1,72,384]{2,1,0:T(8,128)(2,1)} %get-tuple-element.113), channel_id=13, replica_groups=mesh['dp'=8,'mp'=4] {'dp'}, dimensions={1}, use_global_device_ids=true | all-gather | bytes 497664 | tf_op jit(solution)/shard_map/all_gather | solution.py:101
  522.3 32.5 %all_gather.114 = bf16[512,576]{1,0:T(8,128)(2,1)} all-gather(bf16[128,576]{1,0:T(8,128)(2,1)S(1)} %reshape.390), channel_id=1, replica_groups=mesh['dp'=8,'mp'=4] {'mp'}, dimensions={0}, use_global_device_ids=true | all-gather | bytes 737280 | tf_op jit(solution)/shard_map/all_gather | solution.py:122
  556.2 8.1 all_gather.110
  571.3 24.8 %reduce-scatter.45.cloned.1.call-done = bf16[128,576]{1,0:T(8,128)(2,1)} async-done(((bf16[512,576]{1,0:T(8,128)(2,1)}), bf16[128,576]{1,0:T(8,128)(2,1)}) %reduce-scatter.45.cloned.1.call-update) | async-done | bytes 147472 | tf_op jit(solution)/shard_map/reduce_scatter | solution.py:108
  598.9 8.0 all_gather.115
  642.1 9.6 reduce-scatter.47.cloned.1.call-done
  654.0 20.2 %reduce-scatter.49.cloned.1.call-done = bf16[128,192]{1,0:T(8,128)(2,1)} async-done(((bf16[512,192]{1,0:T(8,128)(2,1)}), bf16[128,192]{1,0:T(8,128)(2,1)}) %reduce-scatter.49.cloned.1.call-update) | async-done | bytes 49168
  676.8 8.2 all_to_all.163
  690.1 22.9 %reduce-scatter.51.cloned.1.call-done = bf16[128,576]{1,0:T(8,128)(2,1)} async-done(((bf16[512,576]{1,0:T(8,128)(2,1)}), bf16[128,576]{1,0:T(8,128)(2,1)}) %reduce-scatter.51.cloned.1.call-update) | async-done | bytes 147472 | tf_op jit(solution)/shard_map/reduce_scatter | solution.py:108
  716.9 8.0 all_gather.116
  730.3 22.4 %reduce-scatter.53.cloned.1.call-done = bf16[128,576]{1,0:T(8,128)(2,1)} async-done(((bf16[512,576]{1,0:T(8,128)(2,1)}), bf16[128,576]{1,0:T(8,128)(2,1)}) %reduce-scatter.53.cloned.1.call-update) | async-done | bytes 147472 | tf_op jit(solution)/shard_map/reduce_scatter | solution.py:108
  755.5 8.0 all_gather.117
  798.8 10.3 reduce-scatter.55.cloned.1.call-done
  812.9 18.7 %reduce-scatter.57.cloned.1.call-done = bf16[128,192]{1,0:T(8,128)(2,1)} async-done(((bf16[512,192]{1,0:T(8,128)(2,1)}), bf16[128,192]{1,0:T(8,128)(2,1)}) %reduce-scatter.57.cloned.1.call-update) | async-done | bytes 49168
  955.7 14.7 %all-to-all-done.12 = bf16[8,72,768]{2,1,0:T(8,128)(2,1)S(1)} async-done(((bf16[8,72,768]{2,1,0:T(8,128)(2,1)}), bf16[8,72,768]{2,1,0:T(8,128)(2,1)S(1)}, u32[]{:S(2)}, u32[]{:S(2)}) %all-to-all-start.12) | async-done | bytes 884768 | tf_op jit(solution)/shard_map/all_to_all | solution.py:27
  989.9 41.8 %all-reduce = (f32[2,576]{1,0:T(2,128)}, f32[2,576]{1,0:T(2,128)}) all-reduce(f32[2,576]{1,0:T(2,128)S(1)} %pad_maximum_fusion.19, f32[2,576]{1,0:T(2,128)S(1)} %pad_maximum_fusion.20), channel_id=1, replica_groups=mesh['dp'=8,'mp'=4] {'dp','mp'}, use_global_device_ids=true, to_apply=%region_30.31 | all-reduce | flops 2304 | bytes 18432 | tf_op jit(solution)/shard_map/psum | solution.py:402
  (521 shorter events, 326.2 us)
Async XLA Ops:
  8.0 353.4 %copy-start.86 = (f32[576]{0:T(1024)}, f32[576]{0:T(1024)S(1)}, u32[]{:S(2)}) copy-start(f32[576]{0:T(1024)S(1)} %get-tuple-element.76) | copy-start | bytes 6916
  114.0 8.5 all-to-all-start
  119.8 532.9 %copy-start.45 = (f32[128,64]{0,1:T(8,128)}, f32[128,64]{0,1:T(8,128)S(1)}, u32[]{:S(2)}) copy-start(f32[128,64]{0,1:T(8,128)S(1)} %get-tuple-element.137) | copy-start | bytes 98308
  136.9 29.9 %all-to-all-start.1 = ((bf16[128,4,144]{0,2,1:T(8,128)(2,1)}), bf16[128,4,144]{0,2,1:T(8,128)(2,1)S(1)}, u32[]{:S(2)}, u32[]{:S(2)}) async-start(bf16[128,4,144]{0,2,1:T(8,128)(2,1)} %bitcast.24), calls=%async_computation.1 | async-start | bytes 294912 | tf_op jit(solution)/shard_map/all_to_all | solution.py:118
  140.6 105.3 %reduce-scatter.37.cloned.1.call-start = ((), (), s32[]{:S(2)}) async-start(), calls=%async_computation.28 | async-start | bytes 819200 | tf_op jit(solution)/shard_map/reduce_scatter | solution.py:108
  168.4 191.3 %reduce-scatter.39.cloned.1.call-start = ((), (), s32[]{:S(2)}) async-start(), calls=%async_computation.29 | async-start | bytes 819200 | tf_op jit(solution)/shard_map/reduce_scatter | solution.py:108
  169.1 112.0 %copy-start.79 = (f32[576]{0:T(1024)}, f32[576]{0:T(1024)S(1)}, u32[]{:S(2)}) copy-start(f32[576]{0:T(1024)S(1)} %get-tuple-element.75) | copy-start | bytes 6916
  169.1 428.7 %copy-start.81 = (f32[576]{0:T(1024)}, f32[576]{0:T(1024)S(1)}, u32[]{:S(2)}) copy-start(f32[576]{0:T(1024)S(1)} %get-tuple-element.74) | copy-start | bytes 6916
  410.1 30.3 %all-to-all-start.3 = ((bf16[128,4,144]{0,2,1:T(8,128)(2,1)}), bf16[128,4,144]{0,2,1:T(8,128)(2,1)S(1)}, u32[]{:S(2)}, u32[]{:S(2)}) async-start(bf16[128,4,144]{0,2,1:T(8,128)(2,1)} %bitcast.49), calls=%async_computation.3 | async-start | bytes 294912 | tf_op jit(solution)/shard_map/all_to_all | solution.py:118
  413.7 141.1 %reduce-scatter.41.cloned.1.call-start = ((), (), s32[]{:S(2)}) async-start(), calls=%async_computation.30 | async-start | bytes 819200 | tf_op jit(solution)/shard_map/reduce_scatter | solution.py:108
  442.0 112.8 %copy-start.36 = (bf16[128,576]{1,0:T(8,128)(2,1)S(1)}, bf16[128,576]{1,0:T(8,128)(2,1)}, u32[]{:S(2)}) copy-start(bf16[128,576]{1,0:T(8,128)(2,1)} %reduce-scatter.39.cloned.1.call-done) | copy-start | bytes 442372
  442.0 154.1 %reduce-scatter.45.cloned.1.call-start = ((), (), s32[]{:S(2)}) async-start(), calls=%async_computation.32 | async-start | bytes 819200 | tf_op jit(solution)/shard_map/reduce_scatter | solution.py:108
  442.2 112.6 %copy-start.21 = (bf16[128,576]{1,0:T(8,128)(2,1)}, bf16[128,576]{1,0:T(8,128)(2,1)S(1)}, u32[]{:S(2)}) copy-start(bf16[128,576]{1,0:T(8,128)(2,1)S(1)} %reshape.390) | copy-start | bytes 442372
  608.9 7.9 all-to-all-start.4
  613.0 38.7 %reduce-scatter.47.cloned.1.call-start = ((), (), s32[]{:S(2)}) async-start(), calls=%async_computation.33 | async-start | bytes 327680
  631.1 43.1 %reduce-scatter.49.cloned.1.call-start = ((), (), s32[]{:S(2)}) async-start(), calls=%async_computation.34 | async-start | bytes 327680
  638.5 74.4 %reduce-scatter.51.cloned.1.call-start = ((), (), s32[]{:S(2)}) async-start(), calls=%async_computation.35 | async-start | bytes 819200 | tf_op jit(solution)/shard_map/reduce_scatter | solution.py:108
  690.0 62.7 %reduce-scatter.53.cloned.1.call-start = ((), (), s32[]{:S(2)}) async-start(), calls=%async_computation.36 | async-start | bytes 819200 | tf_op jit(solution)/shard_map/reduce_scatter | solution.py:108
  766.3 7.9 all-to-all-start.6
  770.4 38.7 %reduce-scatter.55.cloned.1.call-start = ((), (), s32[]{:S(2)}) async-start(), calls=%async_computation.37 | async-start | bytes 327680
  788.6 43.1 %reduce-scatter.57.cloned.1.call-start = ((), (), s32[]{:S(2)}) async-start(), calls=%async_computation.38 | async-start | bytes 327680
  834.2 9.8 all-to-all-start.7
  844.0 15.3 %all-to-all-start.15 = ((bf16[8,384,72]{1,2,0:T(8,128)(2,1)}), bf16[8,384,72]{1,2,0:T(8,128)(2,1)}, u32[]{:S(2)}, u32[]{:S(2)}) async-start(bf16[8,384,72]{1,2,0:T(8,128)(2,1)} %bitcast.445), calls=%async_computation.15 | async-start | bytes 884736 | tf_op jit(solution)/shard_map/all_to_all | solution.py:27
  859.4 12.7 %all-to-all-start.11 = ((bf16[8,144,72]{2,1,0:T(8,128)(2,1)}), bf16[8,144,72]{2,1,0:T(8,128)(2,1)}, u32[]{:S(2)}, u32[]{:S(2)}) async-start(bf16[8,144,72]{2,1,0:T(8,128)(2,1)} %bitcast.430), calls=%async_computation.11 | async-start | bytes 589824 | tf_op jit(solution)/shard_map/all_to_all | solution.py:27
  872.1 26.2 %all-to-all-start.13 = ((bf16[8,72,768]{2,1,0:T(8,128)(2,1)}), bf16[8,72,768]{2,1,0:T(8,128)(2,1)}, u32[]{:S(2)}, u32[]{:S(2)}) async-start(bf16[8,72,768]{2,1,0:T(8,128)(2,1)} %bitcast.438), calls=%async_computation.13 | async-start | bytes 1769472 | tf_op jit(solution)/shard_map/all_to_all | solution.py:27
  878.6 107.2 %reduce-scatter.59.cloned.1.call-start = ((), (), s32[]{:S(2)}) async-start(), calls=%async_computation.39 | async-start | bytes 819200 | tf_op jit(solution)/shard_map/reduce_scatter | solution.py:108
  883.3 103.5 %reduce-scatter.43.cloned.1.call-start = ((), (), s32[]{:S(2)}) async-start(), calls=%async_computation.31 | async-start | bytes 819200 | tf_op jit(solution)/shard_map/reduce_scatter | solution.py:108
  902.9 12.9 %all-to-all-start.9 = ((bf16[8,72,240]{2,1,0:T(8,128)(2,1)}), bf16[8,72,240]{2,1,0:T(8,128)(2,1)}, u32[]{:S(2)}, u32[]{:S(2)}) async-start(bf16[8,72,240]{2,1,0:T(8,128)(2,1)} %bitcast.111), calls=%async_computation.9 | async-start | bytes 589824 | tf_op jit(solution)/shard_map/all_to_all | solution.py:27
  915.8 16.2 %all-to-all-start.14 = ((bf16[8,384,72]{1,2,0:T(8,128)(2,1)}), bf16[8,384,72]{1,2,0:T(8,128)(2,1)S(1)}, u32[]{:S(2)}, u32[]{:S(2)}) async-start(bf16[8,384,72]{1,2,0:T(8,128)(2,1)} %bitcast.446), calls=%async_computation.14 | async-start | bytes 884736 | tf_op jit(solution)/shard_map/all_to_all | solution.py:27
  931.9 12.2 %all-to-all-start.10 = ((bf16[8,144,72]{2,1,0:T(8,128)(2,1)}), bf16[8,144,72]{2,1,0:T(8,128)(2,1)}, u32[]{:S(2)}, u32[]{:S(2)}) async-start(bf16[8,144,72]{2,1,0:T(8,128)(2,1)} %bitcast.431), calls=%async_computation.10 | async-start | bytes 589824 | tf_op jit(solution)/shard_map/all_to_all | solution.py:27
  944.1 26.3 %all-to-all-start.12 = ((bf16[8,72,768]{2,1,0:T(8,128)(2,1)}), bf16[8,72,768]{2,1,0:T(8,128)(2,1)S(1)}, u32[]{:S(2)}, u32[]{:S(2)}) async-start(bf16[8,72,768]{2,1,0:T(8,128)(2,1)} %bitcast.121), calls=%async_computation.12 | async-start | bytes 1769472 | tf_op jit(solution)/shard_map/all_to_all | solution.py:27
  970.4 13.1 %all-to-all-start.8 = ((bf16[8,72,240]{2,1,0:T(8,128)(2,1)}), bf16[8,72,240]{2,1,0:T(8,128)(2,1)S(1)}, u32[]{:S(2)}, u32[]{:S(2)}) async-start(bf16[8,72,240]{2,1,0:T(8,128)(2,1)} %bitcast.109), calls=%async_computation.8 | async-start | bytes 589824 | tf_op jit(solution)/shard_map/all_to_all | solution.py:27
  (114 other events, 2328.7 us)
Sparse Core Ops, SparseCore 0:
  168.5 32.0 reduce-scatter.36
  285.1 24.5 reduce-scatter.38
  442.1 31.6 reduce-scatter.40
  571.5 24.6 reduce-scatter.44
  631.3 20.3 reduce-scatter.46
  654.1 20.0 reduce-scatter.48
  690.1 22.7 reduce-scatter.50
  730.4 22.3 reduce-scatter.52
  788.7 20.3 reduce-scatter.54
  811.5 20.0 reduce-scatter.56
  883.4 24.3 reduce-scatter.58
  910.2 22.5 reduce-scatter.42
where the time goes:
time: 1050 us; the launch traced here: 1040 us
  blocking collectives  584 us (56%)
  waiting for transfers between devices  181 us (17%)
  matrix products  77.4 us (7%)
  starting transfers between devices  74.5 us (7%)
  local copies, waits for them, and re-layouts  53.8 us (5%)
  other arithmetic  51.1 us (5%)
  between operations  17.2 us (2%)
    all_gather x4, blocking collectives, norm_in(): normed_all = lax.all_gather(normed, 'mp', axis=0, tiled=True)  93.1 us
    reduce_scatter x8, waiting for transfers between devices, share_sum(): lax.psum_scatter(partial_value.astype(jnp.bfloat16), 'mp', scatter_dimens...  70.1 us
    unnamed x16, waiting for transfers between devices  59 us
    all_gather x4, blocking collectives, spread_grad(): lax.all_gather(gradient.astype(jnp.bfloat16), 'mp', axis=0, tiled=True)  56.6 us
    all_gather x2, blocking collectives, feed_gather(): lax.all_gather(up_part, 'dp', axis=0, tiled=True)  52.5 us
    all_gather x2, blocking collectives, feed_gather(): lax.all_gather(down_part, 'dp', axis=1, tiled=True)  51.5 us
    all_gather x2, blocking collectives, feed_gather(): lax.all_gather(gate_part, 'dp', axis=0, tiled=True)  51.3 us
    all_gather x2, blocking collectives, attend_gather(): lax.all_gather(mix_part, 'dp', axis=1, tiled=True)  51 us
  transfers between devices with their start and end apart: 26, of which 19 were waited for; matrix products, arithmetic and copies ran while one was open for 8% of the time, Pallas kernels for 0%

commit v1 on v0

v1 whole, which is shorter than its diff:
```python
import functools
import math

import jax
import jax.numpy as jnp
from jax import lax
from jax.experimental import pallas as pl
from jax.experimental.pallas import tpu as pltpu
from jax.sharding import PartitionSpec as P

HEADS = 9
KV_HEADS = 3
HEAD_DIM = 64
LAYERS = 2


norm_eps = 1e-05
rope_base = 100000.0
masked_value = -1e30


def push_kernel(axis, peers, n_ag, n_a2a, *refs):
    count = n_ag + n_a2a
    ins, outs = refs[:count], refs[count : 2 * count]
    send_sem, recv_sem, local_sem = refs[2 * count :]
    me = lax.axis_index(axis)
    barrier = pltpu.get_barrier_semaphore()
    for step in range(1, peers):
        pl.semaphore_signal(
            barrier,
            inc=1,
            device_id={axis: lax.rem(me + step, peers)},
            device_id_type=pl.DeviceIdType.MESH,
        )
    pl.semaphore_wait(barrier, peers - 1)
    copies = []
    for step in range(1, peers):
        peer = lax.rem(me + step, peers)
        for i in range(count):
            copy = pltpu.make_async_remote_copy(
                src_ref=ins[i] if i < n_ag else ins[i].at[peer],
                dst_ref=outs[i].at[me],
                send_sem=send_sem.at[i, step],
                recv_sem=recv_sem.at[i, step],
                device_id={axis: peer},
                device_id_type=pl.DeviceIdType.MESH,
            )
            copy.start()
            copies.append(copy)
    for i in range(count):
        local = pltpu.make_async_copy(
            ins[i] if i < n_ag else ins[i].at[me], outs[i].at[me], local_sem.at[i]
        )
        local.start()
        copies.append(local)
    for copy in copies:
        copy.wait()


def exchange(number, axis, whole=(), split=()):
    peers = lax.axis_size(axis)
    count = len(whole) + len(split)
    shapes = [jax.ShapeDtypeStruct((peers, *a.shape), a.dtype) for a in whole]
    shapes += [jax.ShapeDtypeStruct(a.shape, a.dtype) for a in split]
    size = sum(math.prod(s.shape) * s.dtype.itemsize for s in shapes)
    space = pltpu.VMEM if size < 6_000_000 else pl.ANY
    return pl.pallas_call(
        functools.partial(push_kernel, axis, peers, len(whole), len(split)),
        out_shape=shapes,
        in_specs=[pl.BlockSpec(memory_space=space)] * count,
        out_specs=[pl.BlockSpec(memory_space=space)] * count,
        scratch_shapes=[
            pltpu.SemaphoreType.DMA((count, peers)),
            pltpu.SemaphoreType.DMA((count, peers)),
            pltpu.SemaphoreType.DMA((count,)),
        ],
        compiler_params=pltpu.CompilerParams(
            collective_id=number, has_side_effects=True, vmem_limit_bytes=40 * 1024 * 1024
        ),
        name="push_" + axis,
    )(*whole, *split)


def doc_positions(seg_ids):
    length_all = seg_ids.shape[-1]
    token_index = jnp.arange(length_all, dtype=jnp.int32)
    starts = jnp.concatenate(
        [token_index[..., :1] == 0, seg_ids[..., 1:] != seg_ids[..., :-1]], axis=-1
    )
    doc_start = lax.cummax(jnp.where(starts, token_index, 0), axis=seg_ids.ndim - 1)
    return token_index - doc_start


def rope_tables(positions):
    half_dim = HEAD_DIM // 2
    exponents = jnp.arange(half_dim, dtype=jnp.float32) * (2.0 / HEAD_DIM)
    inverse = jnp.exp(-math.log(rope_base) * exponents)
    angles = positions.astype(jnp.float32)[..., None] * inverse
    cosine = jnp.cos(angles)
    sine = jnp.sin(angles)
    return (jnp.concatenate([cosine, cosine], axis=-1), jnp.concatenate([sine, sine], axis=-1))


def rotate(values, cosine, sine):
    half_dim = values.shape[-1] // 2
    turned = jnp.concatenate([-values[..., half_dim:], values[..., :half_dim]], axis=-1)
    return values * cosine[..., None, :] + turned * sine[..., None, :]


def matmul_f32(left, right):
    return jnp.dot(left, right, preferred_element_type=jnp.float32)


def inner_rows(left, right):
    return lax.dot_general(
        left, right, (((0,), (0,)), ((), ())), preferred_element_type=jnp.float32
    )


def inner_cols(left, right):
    return lax.dot_general(
        left, right, (((1,), (1,)), ((), ())), preferred_element_type=jnp.float32
    )


def norm_in(residual, gain):
    rows_f32 = residual.astype(jnp.bfloat16).astype(jnp.float32)
    row_scale = lax.rsqrt(jnp.mean(rows_f32 * rows_f32, axis=1, keepdims=True) + norm_eps)
    normed = (rows_f32 * row_scale * gain.astype(jnp.float32)).astype(jnp.bfloat16)
    return (rows_f32, row_scale, normed)


def summed(pieces):
    return jnp.sum(pieces.astype(jnp.float32), axis=0)


def columns_over(gathered):
    peers, rows, width = gathered.shape
    return jnp.moveaxis(gathered, 0, 1).reshape(rows, peers * width)


def norm_back(grad_normed, rows_f32, row_scale, gain):
    width = rows_f32.shape[1]
    gain_f32 = gain.astype(jnp.float32)
    cubed = row_scale * row_scale * row_scale
    inner = jnp.sum(grad_normed * gain_f32 * rows_f32, axis=1, keepdims=True)
    resid_grad = gain_f32 * row_scale * grad_normed - rows_f32 * cubed * inner / width
    gain_term = jnp.sum(grad_normed * rows_f32 * row_scale, axis=0)
    return (resid_grad, gain_term)


def head_views(query_turned, keys_all, values_all):
    own_rows = query_turned.shape[0]
    group_size = HEADS // KV_HEADS
    query_heads = query_turned.reshape(own_rows, KV_HEADS, group_size, HEAD_DIM)
    key_heads = keys_all.reshape(keys_all.shape[0], KV_HEADS, HEAD_DIM)
    value_heads = values_all.reshape(values_all.shape[0], KV_HEADS, HEAD_DIM)
    return (query_heads, key_heads, value_heads)


def masked_logits(query_heads, key_heads, allowed):
    scores = jnp.einsum(
        "qkgd,tkd->kgqt", query_heads, key_heads, preferred_element_type=jnp.float32
    )
    return jnp.where(allowed, scores * (1.0 / math.sqrt(HEAD_DIM)), masked_value)


def attend(query_turned, keys_all, values_all, allowed):
    query_heads, key_heads, value_heads = head_views(query_turned, keys_all, values_all)
    logits = masked_logits(query_heads, key_heads, allowed)
    row_max = jnp.max(logits, axis=3, keepdims=True)
    raised = jnp.exp(logits - row_max)
    row_total = jnp.sum(raised, axis=3, keepdims=True)
    weights_low = (raised / row_total).astype(jnp.bfloat16)
    mixed = jnp.einsum(
        "kgqt,tkd->qkgd", weights_low, value_heads, preferred_element_type=jnp.float32
    )
    return (mixed.reshape(query_turned.shape[0], -1), row_max + jnp.log(row_total))


def attend_back(query_turned, keys_all, values_all, allowed, log_total, grad_mixed):
    query_heads, key_heads, value_heads = head_views(query_turned, keys_all, values_all)
    logits = masked_logits(query_heads, key_heads, allowed)
    weights = jnp.exp(logits - log_total)
    grad_heads = grad_mixed.reshape(query_heads.shape)
    grad_weights = jnp.einsum(
        "qkgd,tkd->kgqt", grad_heads, value_heads, preferred_element_type=jnp.float32
    )
    delta = jnp.sum(weights * grad_weights, axis=3, keepdims=True)
    grad_scores = (weights * (grad_weights - delta) * (1.0 / math.sqrt(HEAD_DIM))).astype(
        jnp.bfloat16
    )
    grad_query = jnp.einsum(
        "kgqt,tkd->qkgd", grad_scores, key_heads, preferred_element_type=jnp.float32
    )
    grad_keys = jnp.einsum(
        "kgqt,qkgd->tkd", grad_scores, query_heads, preferred_element_type=jnp.float32
    )
    grad_values = jnp.einsum(
        "kgqt,qkgd->tkd",
        weights.astype(jnp.bfloat16),
        grad_heads,
        preferred_element_type=jnp.float32,
    )
    row_count = keys_all.shape[0]
    return (
        grad_query.reshape(query_turned.shape[0], -1),
        grad_keys.reshape(row_count, -1),
        grad_values.reshape(row_count, -1),
    )


def on_device(
    block_input,
    segments,
    attend_gain,
    query_weight,
    key_weight,
    value_weight,
    mix_weight,
    feed_gain,
    gate_weight,
    up_weight,
    down_weight,
    cotangent,
):
    bf16, f32 = jnp.bfloat16, jnp.float32
    width = block_input.shape[1] // 2
    own_rows = block_input.shape[0] * 2
    mp = lax.axis_size("mp")
    dp = lax.axis_size("dp")
    row_count = own_rows * mp
    first_row = lax.axis_index("mp") * own_rows
    qw, kw, ff = query_weight.shape[2], key_weight.shape[2], gate_weight.shape[2]
    depth = query_weight.shape[1]
    aw = 2 * qw + 2 * kw
    packed = jnp.concatenate(
        [
            query_weight,
            key_weight,
            value_weight,
            jnp.swapaxes(mix_weight, 1, 2),
            gate_weight,
            up_weight,
            jnp.swapaxes(down_weight, 1, 2),
        ],
        axis=2,
    )
    total_width = packed.shape[2]
    packed = packed.reshape(LAYERS * depth, total_width)
    residual = block_input.reshape(own_rows, width).astype(f32)
    rows_f32, row_scale, normed = norm_in(residual, attend_gain[0])
    (weights,) = exchange(0, "dp", [packed])
    weights = jnp.moveaxis(weights.reshape(dp, LAYERS, depth, total_width), 1, 0)
    weights = weights.reshape(LAYERS, width, total_width)
    attend_all, normed_all = exchange(
        1, "mp", [weights[:, :, :aw].reshape(LAYERS * width, aw), normed]
    )
    attend_all = attend_all.reshape(mp, LAYERS, width, aw)
    attend_full, feed_full = ([], [])
    for layer in range(LAYERS):
        part = attend_all[:, layer]
        attend_full.append(
            (
                columns_over(part[:, :, :qw]),
                columns_over(part[:, :, qw : qw + kw]),
                columns_over(part[:, :, qw + kw : qw + 2 * kw]),
                columns_over(part[:, :, qw + 2 * kw :]),
            )
        )
        feed = weights[layer, :, aw:]
        feed_full.append((feed[:, :ff], feed[:, ff : 2 * ff], feed[:, 2 * ff :]))

    seg_ids = segments[0]
    positions = doc_positions(seg_ids)
    my_segs = lax.dynamic_slice_in_dim(seg_ids, first_row, own_rows, 0)
    cos_all, sin_all = rope_tables(positions)
    cosine = lax.dynamic_slice_in_dim(cos_all, first_row, own_rows, 0)
    sine = lax.dynamic_slice_in_dim(sin_all, first_row, own_rows, 0)
    key_index = jnp.arange(row_count, dtype=jnp.int32)
    query_index = first_row + jnp.arange(own_rows, dtype=jnp.int32)
    allowed = (key_index[None, :] <= query_index[:, None]) & (seg_ids[None, :] == my_segs[:, None])

    attend_saved = []
    feed_saved = []
    for layer in range(LAYERS):
        query_full, key_full, value_full, mix_turned = attend_full[layer]
        if layer > 0:
            rows_f32, row_scale, normed = norm_in(residual, attend_gain[layer])
            (normed_all,) = exchange(10 + layer, "mp", [normed])
        normed_all = normed_all.reshape(row_count, width)
        query_rows = matmul_f32(normed, query_full).astype(bf16).astype(f32)
        key_rows = matmul_f32(normed_all, key_full).astype(bf16).astype(f32)
        values_all = matmul_f32(normed_all, value_full).astype(bf16)
        query_turned = rotate(query_rows.reshape(own_rows, HEADS, HEAD_DIM), cosine, sine)
        query_turned = query_turned.reshape(own_rows, -1).astype(bf16)
        keys_all = rotate(key_rows.reshape(row_count, KV_HEADS, HEAD_DIM), cos_all, sin_all)
        keys_all = keys_all.reshape(row_count, -1).astype(bf16)
        mixed, log_total = attend(query_turned, keys_all, values_all, allowed)
        mixed = mixed.astype(bf16)
        residual = residual + inner_cols(mixed, mix_turned)
        attend_saved.append(
            (
                rows_f32,
                row_scale,
                normed_all,
                query_turned,
                keys_all,
                values_all,
                log_total,
                mixed,
            )
        )
        rows_two, scale_two, normed_two = norm_in(residual, feed_gain[layer])
        (normed_two,) = exchange(20 + layer, "mp", [normed_two])
        normed_two = normed_two.reshape(row_count, width)
        gate_full, up_full, down_turned = feed_full[layer]
        gate_out = matmul_f32(normed_two, gate_full)
        up_out = matmul_f32(normed_two, up_full)
        hidden = (jax.nn.silu(gate_out) * up_out).astype(bf16)
        part = inner_cols(hidden, down_turned).astype(bf16).reshape(mp, own_rows, width)
        (part,) = exchange(30 + layer, "mp", (), [part])
        residual = residual + summed(part)
        feed_saved.append((rows_two, scale_two, normed_two, gate_out, up_out, hidden))
    block_output = residual.astype(bf16).reshape(own_rows // 2, 2 * width)

    grad_resid = cotangent.reshape(own_rows, width).astype(f32)
    attend_terms = [None] * LAYERS
    feed_terms = [None] * LAYERS
    grads = [None] * LAYERS
    feed_grads = [None] * LAYERS

    def attend_grads(layer, received):
        grad_all, mixed_cols, dqkv_cols = [a.reshape(row_count, -1) for a in received]
        normed_all = attend_saved[layer][2]
        return jnp.concatenate(
            [inner_rows(normed_all, dqkv_cols), inner_rows(grad_all, mixed_cols)], axis=1
        )

    late = None
    for layer in range(LAYERS - 1, -1, -1):
        rows_two, scale_two, normed_two, gate_out, up_out, hidden = feed_saved[layer]
        gate_full, up_full, down_turned = feed_full[layer]
        got = exchange(
            40 + layer,
            "mp",
            [grad_resid.astype(bf16)] + ([late[0]] if late else []),
            late[1:] if late else [],
        )
        grad_full = got[0].reshape(row_count, width)
        if late:
            grads[layer + 1] = attend_grads(layer + 1, got[1:])
        grad_hidden = matmul_f32(grad_full, down_turned)
        down_term = inner_rows(grad_full, hidden)
        sigmoid_gate = jax.nn.sigmoid(gate_out)
        grad_gate = (
            grad_hidden * up_out * sigmoid_gate * (1.0 + gate_out * (1.0 - sigmoid_gate))
        ).astype(bf16)
        grad_up = (grad_hidden * gate_out * sigmoid_gate).astype(bf16)
        grad_normed = (inner_cols(grad_gate, gate_full) + inner_cols(grad_up, up_full)).astype(bf16)
        (part,) = exchange(50 + layer, "mp", (), [grad_normed.reshape(mp, own_rows, width)])
        feed_grads[layer] = jnp.concatenate(
            [inner_rows(normed_two, grad_gate), inner_rows(normed_two, grad_up), down_term], axis=1
        )
        resid_grad, feed_terms[layer] = norm_back(
            summed(part), rows_two, scale_two, feed_gain[layer]
        )
        grad_resid = grad_resid + resid_grad
        (
            rows_f32,
            row_scale,
            normed_all,
            query_turned,
            keys_all,
            values_all,
            log_total,
            mixed,
        ) = attend_saved[layer]
        query_full, key_full, value_full, mix_turned = attend_full[layer]
        grad_low = grad_resid.astype(bf16)
        grad_mixed = matmul_f32(grad_low, mix_turned).astype(bf16)
        grad_query, grad_keys, grad_values = attend_back(
            query_turned, keys_all, values_all, allowed, log_total, grad_mixed
        )
        key_value = jnp.concatenate([grad_keys, grad_values], axis=1).astype(bf16)
        (key_value,) = exchange(
            60 + layer, "mp", (), [key_value.reshape(mp, own_rows, 2 * mp * kw)]
        )
        key_value = summed(key_value)
        query_back = rotate(grad_query.reshape(own_rows, HEADS, HEAD_DIM), cosine, -sine)
        query_back = query_back.reshape(own_rows, -1).astype(bf16)
        key_back = rotate(
            key_value[:, : mp * kw].reshape(own_rows, KV_HEADS, HEAD_DIM), cosine, -sine
        )
        key_back = key_back.reshape(own_rows, -1).astype(bf16)
        value_back = key_value[:, mp * kw :].astype(bf16)
        grad_normed = (
            inner_cols(query_back, query_full)
            + inner_cols(key_back, key_full)
            + inner_cols(value_back, value_full)
        )
        resid_grad, attend_terms[layer] = norm_back(
            grad_normed, rows_f32, row_scale, attend_gain[layer]
        )
        grad_resid = grad_resid + resid_grad
        dqkv = jnp.concatenate(
            [a.reshape(own_rows, mp, -1) for a in (query_back, key_back, value_back)], axis=2
        )
        late = (
            grad_low,
            jnp.moveaxis(mixed.reshape(own_rows, mp, qw), 1, 0),
            jnp.moveaxis(dqkv, 1, 0),
        )
    gains = jnp.concatenate([jnp.stack(attend_terms), jnp.stack(feed_terms)], axis=0)
    gains = jnp.concatenate([gains, jnp.zeros((8 - 2 * LAYERS, width), f32)], axis=0)
    got = exchange(2, "mp", [late[0], gains], late[1:])
    grads[0] = attend_grads(0, (got[0], got[2], got[3]))
    gains = summed(got[1])
    grad_pack = jnp.stack(
        [jnp.concatenate([grads[i], feed_grads[i]], axis=1).astype(bf16) for i in range(LAYERS)]
    )
    grad_pack = jnp.moveaxis(grad_pack.reshape(LAYERS, dp, depth, total_width), 1, 0)
    gains, grad_pack = exchange(
        3, "dp", [gains], [grad_pack.reshape(dp, LAYERS * depth, total_width)]
    )
    gains = summed(gains)
    total = summed(grad_pack).reshape(LAYERS, depth, total_width)
    input_grad = grad_resid.reshape(own_rows // 2, 2 * width)
    return (
        block_output,
        input_grad,
        gains[:LAYERS],
        total[:, :, :qw],
        total[:, :, qw : qw + kw],
        total[:, :, qw + kw : qw + 2 * kw],
        jnp.swapaxes(total[:, :, qw + 2 * kw : aw], 1, 2),
        gains[LAYERS : 2 * LAYERS],
        total[:, :, aw : aw + ff],
        total[:, :, aw + ff : aw + 2 * ff],
        jnp.swapaxes(total[:, :, aw + 2 * ff :], 1, 2),
    )


def solution(mesh):
    in_specs = (
        P(("dp", "mp"), None),
        P("dp", None),
        P(),
        P(None, "dp", "mp"),
        P(None, "dp", "mp"),
        P(None, "dp", "mp"),
        P(None, "mp", "dp"),
        P(),
        P(None, "dp", "mp"),
        P(None, "dp", "mp"),
        P(None, "mp", "dp"),
        P(("dp", "mp"), None),
    )
    out_specs = (
        P(("dp", "mp"), None),
        P(("dp", "mp"), None),
        P(),
        P(None, "dp", "mp"),
        P(None, "dp", "mp"),
        P(None, "dp", "mp"),
        P(None, "mp", "dp"),
        P(),
        P(None, "dp", "mp"),
        P(None, "dp", "mp"),
        P(None, "mp", "dp"),
    )
    return jax.shard_map(
        on_device, mesh=mesh, in_specs=in_specs, out_specs=out_specs, check_vma=False
    )
```

time: 1050 us -> 579 us (0.55)
  blocking collectives: 584 us -> 0 us
  Pallas kernels: 0 us -> 342 us
  waiting for transfers between devices: 181 us -> 0 us
  starting transfers between devices: 74.5 us -> 0 us
  local copies, waits for them, and re-layouts: 53.8 us -> 105 us
  other arithmetic: 51.1 us -> 35.7 us
  between operations: 17.2 us -> 3.17 us
    all_gather x26 -> x0, blocking collectives: 526 us -> none  [the longest x4 93.1 us: norm_in(): normed_all = lax.all_gather(normed, 'mp', axis=0, tiled=True)]
    pallas_call x0 -> x15, Pallas kernels: none -> 342 us  [exchange(): pl.pallas_call(functools.partial(push_kernel, axis, peers, len(whole), le...]
    all_to_all x14 -> x0, starting transfers between devices: 73.9 us -> none  [the longest x8 50.3 us: sent_and_summed(): lax.all_to_all(in_blocks(shard, dim, peers), axis, 0, 0, tiled=True)]
    reduce_scatter x8 -> x0, waiting for transfers between devices: 70.1 us -> none  [share_sum(): lax.psum_scatter(partial_value.astype(jnp.bfloat16), 'mp', scatter_dimens...]
    unnamed x16 -> x0, waiting for transfers between devices: 59 us -> none
    all_to_all x14 -> x0, waiting for transfers between devices: 52.1 us -> none  [the longest x8 41.5 us: sent_and_summed(): lax.all_to_all(in_blocks(shard, dim, peers), axis, 0, 0, tiled=True)]
    psum x1 -> x0, blocking collectives: 41.8 us -> none  [on_device(): lax.psum((jnp.stack(attend_terms), jnp.stack(feed_terms)), ('dp', 'mp'))]
    concatenate x7 -> x13, local copies, waits for them, and re-layouts: 1.85 us -> 22.5 us  [the longest x8 13.8 us: on_device(): key_value = jnp.concatenate([grad_keys, grad_values], axis=1).astype(bf16)]
  transfers between devices with their start and end apart: 26 -> 0, of which waited for: 19 -> 0; matrix products, arithmetic and copies ran while one was open for 8% -> 0% of each run, Pallas kernels for 0% -> 0%
where the time goes in v1:
time: 579 us; the launch traced here: 568 us
  Pallas kernels  342 us (59%)
  local copies, waits for them, and re-layouts  105 us (18%)
  matrix products  82.4 us (14%)
  other arithmetic  35.7 us (6%)
    pallas_call x15, Pallas kernels, exchange(): pl.pallas_call(functools.partial(push_kernel, axis, peers, len(whole), le...  342 us
    unnamed x246, local copies, waits for them, and re-layouts  34.3 us
    dot_general x14, matrix products, inner_cols(): lax.dot_general(left, right, (((1,), (1,)), ((), ())), preferred_element_...  21.6 us
    dot_general x10, matrix products, inner_rows(): lax.dot_general(left, right, (((0,), (0,)), ((), ())), preferred_element_...  14.5 us
    dot_general x14, matrix products, matmul_f32(): return jnp.dot(left, right, preferred_element_type=jnp.float32)  14.3 us
    concatenate x8, local copies, waits for them, and re-layouts, on_device(): key_value = jnp.concatenate([grad_keys, grad_values], axis=1).astype(bf16)  13.8 us

profile of v1, /device:TPU:11, one launch (start us, length us, event | category | flops | bytes accessed | tf_op | source)
XLA Modules:
  0.0 568.0 jit_solution(11992842217880194146)
XLA Ops:
  5.5 80.7 %push_dp.2 = bf16[8,144,1536]{2,1,0:T(8,128)(2,1)S(1)} custom-call(bf16[144,1536]{1,0:T(8,128)(2,1)S(1)} %bitcast.446), custom_call_target="tpu_custom_call" | custom-call | tf_op jit(solution)/shard_map/push_dp/pallas_call | solution.py:67
  88.4 48.0 %push_mp.13 = (bf16[4,1152,384]{2,1,0:T(8,128)(2,1)S(1)}, bf16[4,128,576]{2,1,0:T(8,128)(2,1)S(1)}) custom-call(bf16[1152,384]{1,0:T(8,128)(2,1)S(1)} %bitcast.437, bf16[128,576]{1,0:T(8,128)(2,1)S(1)} %multiply_convert_fusion.6.refs_1_), custom_call_target="tpu_custom_call" | custom-call | tf_op jit(solution)/shard_map/push_mp/pallas_call | solution.py:67
  138.6 3.9 copy.297
  156.7 9.6 %push_mp.14 = bf16[4,128,576]{2,1,0:T(8,128)(2,1)S(1)} custom-call(bf16[128,576]{1,0:T(8,128)(2,1)S(1)} %fusion.87.refs_0_), custom_call_target="tpu_custom_call" | custom-call | tf_op jit(solution)/shard_map/push_mp/pallas_call | solution.py:67
  170.5 9.6 %push_mp.15 = bf16[4,128,576]{2,1,0:T(8,128)(2,1)S(1)} custom-call(bf16[4,128,576]{2,1,0:T(8,128)(2,1)S(1)} %bitcast.442), custom_call_target="tpu_custom_call" | custom-call | tf_op jit(solution)/shard_map/push_mp/pallas_call | solution.py:67
  182.0 9.6 %push_mp.16 = bf16[4,128,576]{2,1,0:T(8,128)(2,1)S(1)} custom-call(bf16[128,576]{1,0:T(8,128)(2,1)S(1)} %fusion.97.refs_0_), custom_call_target="tpu_custom_call" | custom-call | tf_op jit(solution)/shard_map/push_mp/pallas_call | solution.py:67
  191.6 3.9 copy.298
  202.7 9.6 %push_mp.17 = bf16[4,128,576]{2,1,0:T(8,128)(2,1)S(1)} custom-call(bf16[128,576]{1,0:T(8,128)(2,1)S(1)} %fusion.107.refs_0_), custom_call_target="tpu_custom_call" | custom-call | tf_op jit(solution)/shard_map/push_mp/pallas_call | solution.py:67
  215.2 9.6 %push_mp.19 = bf16[4,128,576]{2,1,0:T(8,128)(2,1)S(1)} custom-call(bf16[128,576]{1,0:T(8,128)(2,1)S(1)} %reshape.635.refs_0_), custom_call_target="tpu_custom_call" | custom-call | tf_op jit(solution)/shard_map/push_mp/pallas_call | solution.py:67
  224.8 3.2 multiply_convert_fusion.2
  228.8 2.4 convolution_convert_fusion
  234.4 9.6 %push_mp.18 = bf16[4,128,576]{2,1,0:T(8,128)(2,1)S(1)} custom-call(bf16[4,128,576]{2,1,0:T(8,128)(2,1)S(1)} %bitcast.443), custom_call_target="tpu_custom_call" | custom-call | tf_op jit(solution)/shard_map/push_mp/pallas_call | solution.py:67
  248.1 2.4 fusion.12
  253.8 9.6 %push_mp.20 = bf16[4,128,576]{2,1,0:T(8,128)(2,1)S(1)} custom-call(bf16[4,128,576]{2,1,0:T(8,128)(2,1)S(1)} %bitcast.444), custom_call_target="tpu_custom_call" | custom-call | tf_op jit(solution)/shard_map/push_mp/pallas_call | solution.py:67
  268.0 5.7 %fusion.30 = f32[3,64,3,128]{3,1,2,0:T(8,128)} fusion(bf16[512,3,64,1]{0,2,3,1:T(8,128)(2,1)} %bitcast.507, f32[3,512,128,3]{2,1,3,0:T(8,128)} %fusion.158, f32[3,3,128,512]{2,3,1,0:T(8,128)} %copy-done.23, f32[3,3,128]{2,1,0:T(4,128)S(1)} %log_add_fusion.1), kind=kOutput, calls=%fused_computation.73 | convolution fusion | flops 79627904 | bytes 5214720 | tf_op jit(solution)/shard_map/kgqt,tkd->qkgd/dot_general | solution.py:193
  276.7 2.2 fusion.159
  283.5 5.7 fusion.50
  293.8 6.8 %push_mp.21 = bf16[4,128,384]{2,1,0:T(8,128)(2,1)S(1)} custom-call(bf16[4,128,384]{2,1,0:T(8,128)(2,1)S(1)} %pad_maximum_fusion.refs_0_), custom_call_target="tpu_custom_call" | custom-call | tf_op jit(solution)/shard_map/push_mp/pallas_call | solution.py:67
  325.9 22.4 %push_mp.22 = (bf16[4,128,576]{2,1,0:T(8,128)(2,1)S(1)}, bf16[4,128,576]{2,1,0:T(8,128)(2,1)S(1)}, bf16[4,128,144]{2,1,0:T(8,128)(2,1)S(1)}, bf16[4,128,240]{2,1,0:T(8,128)(2,1)S(1)}) custom-call(bf16[128,576]{1,0:T(8,128)(2,1)S(1)} %copy-done.12, bf16[128,576]{1,0:T(8,128)(2,1)S(1)} %copy-done.4, bf16[4,128,144]{2,1,0:T(8,128)(2,1)S(1)} %bitcast.447, ...), custom_call_target="tpu_custom_call" | custom-call | tf_op jit(solution)/shard_map/push_mp/pallas_call | solution.py:67
  348.4 2.7 multiply_convert_fusion
  353.4 2.2 copy.230
  356.7 10.8 %push_mp.23 = bf16[4,128,576]{2,1,0:T(8,128)(2,1)S(1)} custom-call(bf16[4,128,576]{2,1,0:T(8,128)(2,1)S(1)} %bitcast.445), custom_call_target="tpu_custom_call" | custom-call | tf_op jit(solution)/shard_map/push_mp/pallas_call | solution.py:67
  371.8 5.6 fusion.25
  380.4 2.2 fusion.161
  387.2 5.6 fusion.49
  397.4 7.0 %push_mp.24 = bf16[4,128,384]{2,1,0:T(8,128)(2,1)S(1)} custom-call(bf16[4,128,384]{2,1,0:T(8,128)(2,1)S(1)} %pad_maximum_fusion.1.refs_0_), custom_call_target="tpu_custom_call" | custom-call | tf_op jit(solution)/shard_map/push_mp/pallas_call | solution.py:67
  431.4 16.3 %push_mp.25 = (bf16[4,128,576]{2,1,0:T(8,128)(2,1)S(1)}, f32[4,8,576]{2,1,0:T(8,128)S(1)}, bf16[4,128,144]{2,1,0:T(8,128)(2,1)S(1)}, bf16[4,128,240]{2,1,0:T(8,128)(2,1)S(1)}) custom-call(bf16[128,576]{1,0:T(8,128)(2,1)S(1)} %get-tuple-element.91.refs_0_, f32[8,576]{1,0:T(8,128)S(1)} %concatenate.136.refs_1_, bf16[4,128,144]{2,1,0:T(8,128)(2,1)S(1)} %bitcast.448, ...), custom_call_target="tpu_custom_call" | custom-call | tf_op jit(solution)/shard_map/push_mp/pallas_call | solution.py:67
  455.2 2.3 fusion.19
  457.5 2.2 fusion.20
  461.0 4.0 concatenate.149
  471.7 2.6 concatenate.143
  475.3 83.1 %push_dp.3 = (f32[8,8,576]{2,1,0:T(8,128)S(1)}, bf16[8,144,1536]{2,1,0:T(8,128)(2,1)S(1)}) custom-call(f32[8,576]{1,0:T(8,128)S(1)} %copy-done.17, bf16[8,144,1536]{2,1,0:T(8,128)(2,1)S(1)} %bitcast.426), custom_call_target="tpu_custom_call" | custom-call | tf_op jit(solution)/shard_map/push_dp/pallas_call | solution.py:67
  (426 shorter events, 163.8 us)
Async XLA Ops:
  1.7 153.3 %copy-start.27 = (f32[128,576]{1,0:T(8,128)}, f32[128,576]{1,0:T(8,128)S(1)}, u32[]{:S(2)}) copy-start(f32[128,576]{1,0:T(8,128)S(1)} %reshape.654) | copy-start | bytes 884740
  87.0 62.4 %copy-start.93 = (f32[576]{0:T(1024)}, f32[576]{0:T(1024)S(1)}, u32[]{:S(2)}) copy-start(f32[576]{0:T(1024)S(1)} %get-tuple-element.173) | copy-start | bytes 6916
  87.0 69.6 %copy-start.96 = (f32[576]{0:T(1024)}, f32[576]{0:T(1024)S(1)}, u32[]{:S(2)}) copy-start(f32[576]{0:T(1024)S(1)} %get-tuple-element.88) | copy-start | bytes 6916
  87.0 94.8 %copy-start.98 = (f32[576]{0:T(1024)}, f32[576]{0:T(1024)S(1)}, u32[]{:S(2)}) copy-start(f32[576]{0:T(1024)S(1)} %get-tuple-element.174) | copy-start | bytes 6916
  87.1 177.1 %copy-start.95 = (f32[576]{0:T(1024)}, f32[576]{0:T(1024)S(1)}, u32[]{:S(2)}) copy-start(f32[576]{0:T(1024)S(1)} %get-tuple-element.87) | copy-start | bytes 6916
  88.1 60.7 %copy-start.108 = (f32[128]{0:T(128)}, f32[128]{0:T(128)S(1)}, u32[]{:S(2)}) copy-start(f32[128]{0:T(128)S(1)} %get-tuple-element.153) | copy-start | bytes 1540
  153.9 12.4 %copy-start.26 = (bf16[2,8,72,1536]{3,2,1,0:T(8,128)(2,1)S(1)}, bf16[2,8,72,1536]{3,2,1,0:T(8,128)(2,1)}, u32[]{:S(2)}) copy-start(bf16[2,8,72,1536]{3,2,1,0:T(8,128)(2,1)} %copy-done.25) | copy-start | bytes 10616836
  154.9 12.7 %copy-start.83 = (bf16[3,64,3,128]{3,1,2,0:T(8,128)(2,1)}, bf16[3,64,3,128]{3,1,2,0:T(8,128)(2,1)S(1)}, u32[]{:S(2)}) copy-start(bf16[3,64,3,128]{3,1,2,0:T(8,128)(2,1)S(1)} %fusion.48) | copy-start | bytes 442372
  156.0 11.6 %copy-start.47 = (bf16[128,576]{1,0:T(8,128)(2,1)}, bf16[128,576]{1,0:T(8,128)(2,1)S(1)}, u32[]{:S(2)}) copy-start(bf16[128,576]{1,0:T(8,128)(2,1)S(1)} %get-tuple-element.103) | copy-start | bytes 442372
  156.6 11.0 %copy-start.112 = (f32[128]{0:T(128)}, f32[128]{0:T(128)S(1)}, u32[]{:S(2)}) copy-start(f32[128]{0:T(128)S(1)} %get-tuple-element.155) | copy-start | bytes 1540
  181.3 14.2 %copy-start.50 = (bf16[128,576]{1,0:T(8,128)(2,1)}, bf16[128,576]{1,0:T(8,128)(2,1)S(1)}, u32[]{:S(2)}) copy-start(bf16[128,576]{1,0:T(8,128)(2,1)S(1)} %get-tuple-element.100) | copy-start | bytes 442372
  181.8 13.6 %copy-start.111 = (f32[128]{0:T(128)}, f32[128]{0:T(128)S(1)}, u32[]{:S(2)}) copy-start(f32[128]{0:T(128)S(1)} %get-tuple-element.157) | copy-start | bytes 1540
  201.4 12.2 %copy-start.84 = (bf16[3,64,3,128]{3,1,2,0:T(8,128)(2,1)}, bf16[3,64,3,128]{3,1,2,0:T(8,128)(2,1)S(1)}, u32[]{:S(2)}) copy-start(bf16[3,64,3,128]{3,1,2,0:T(8,128)(2,1)S(1)} %fusion.47) | copy-start | bytes 442372
  201.4 10.8 %copy-start.29 = (bf16[576,1152]{1,0:T(8,128)(2,1)S(1)}, bf16[576,1152]{1,0:T(8,128)(2,1)}, u32[]{:S(2)}) copy-start(bf16[576,1152]{1,0:T(8,128)(2,1)} %get-tuple-element.104) | copy-start | bytes 3981316
  202.5 11.2 %copy-start.43 = (bf16[128,576]{1,0:T(8,128)(2,1)}, bf16[128,576]{1,0:T(8,128)(2,1)S(1)}, u32[]{:S(2)}) copy-start(bf16[128,576]{1,0:T(8,128)(2,1)S(1)} %get-tuple-element.98) | copy-start | bytes 442372
  202.5 61.7 %copy-start.110 = (f32[128]{0:T(128)}, f32[128]{0:T(128)S(1)}, u32[]{:S(2)}) copy-start(f32[128]{0:T(128)S(1)} %get-tuple-element.159) | copy-start | bytes 1540
  202.5 61.7 %copy-start.115 = (f32[128]{0:T(128)}, f32[128]{0:T(128)S(1)}, u32[]{:S(2)}) copy-start(f32[128]{0:T(128)S(1)} %get-tuple-element.158) | copy-start | bytes 1540
  202.6 12.5 %copy-start.92 = (bf16[64,1152]{1,0:T(8,128)(2,1)S(1)}, bf16[64,1152]{1,0:T(8,128)(2,1)}, u32[]{:S(2)}) copy-start(bf16[64,1152]{1,0:T(8,128)(2,1)} %param.23) | copy-start | bytes 442372
  253.8 10.6 %copy-start.39 = (bf16[4,576,144]{1,2,0:T(8,128)(2,1)S(1)}, bf16[4,576,144]{1,2,0:T(8,128)(2,1)}, u32[]{:S(2)}) copy-start(bf16[4,576,144]{1,2,0:T(8,128)(2,1)} %copy-done.38) | copy-start | bytes 1990660
  253.8 12.3 %copy-start.82 = (bf16[512,192]{0,1:T(8,128)(2,1)S(1)}, bf16[512,192]{0,1:T(8,128)(2,1)}, u32[]{:S(2)}) copy-start(bf16[512,192]{0,1:T(8,128)(2,1)} %copy-done.81) | copy-start | bytes 589828
  321.6 26.8 %copy-start.32 = (bf16[576,1152]{1,0:T(8,128)(2,1)S(1)}, bf16[576,1152]{1,0:T(8,128)(2,1)}, u32[]{:S(2)}) copy-start(bf16[576,1152]{1,0:T(8,128)(2,1)} %copy-done.31) | copy-start | bytes 3981316
  353.4 14.3 %copy-start.48 = (bf16[128,576]{1,0:T(8,128)(2,1)S(1)}, bf16[128,576]{1,0:T(8,128)(2,1)}, u32[]{:S(2)}) copy-start(bf16[128,576]{1,0:T(8,128)(2,1)} %copy-done.47) | copy-start | bytes 442372
  353.4 14.3 %copy-start.97 = (f32[576]{0:T(1024)S(1)}, f32[576]{0:T(1024)}, u32[]{:S(2)}) copy-start(f32[576]{0:T(1024)} %copy-done.96) | copy-start | bytes 6916
  353.4 14.3 %copy-start.113 = (f32[128]{0:T(128)S(1)}, f32[128]{0:T(128)}, u32[]{:S(2)}) copy-start(f32[128]{0:T(128)} %copy-done.112) | copy-start | bytes 1540
  353.4 14.4 %copy-start.117 = (f32[128]{0:T(128)S(1)}, f32[128]{0:T(128)}, u32[]{:S(2)}) copy-start(f32[128]{0:T(128)} %get-tuple-element.154) | copy-start | bytes 1540
  356.7 11.1 %copy-start.49 = (bf16[128,576]{1,0:T(8,128)(2,1)S(1)}, bf16[128,576]{1,0:T(8,128)(2,1)}, u32[]{:S(2)}) copy-start(bf16[128,576]{1,0:T(8,128)(2,1)} %copy-done.47) | copy-start | bytes 442372
  356.7 11.1 %copy-start.72 = (f32[128,576]{1,0:T(8,128)S(1)}, f32[128,576]{1,0:T(8,128)}, u32[]{:S(2)}) copy-start(f32[128,576]{1,0:T(8,128)} %get-tuple-element.94) | copy-start | bytes 884740
  356.7 12.1 %copy-start.37 = (bf16[4,576,144]{1,2,0:T(8,128)(2,1)S(1)}, bf16[4,576,144]{1,2,0:T(8,128)(2,1)}, u32[]{:S(2)}) copy-start(bf16[4,576,144]{1,2,0:T(8,128)(2,1)} %copy-done.36) | copy-start | bytes 1990660
  356.7 13.1 %copy-start.80 = (bf16[512,192]{0,1:T(8,128)(2,1)S(1)}, bf16[512,192]{0,1:T(8,128)(2,1)}, u32[]{:S(2)}) copy-start(bf16[512,192]{0,1:T(8,128)(2,1)} %convolution_convert_fusion.11) | copy-start | bytes 589828
  394.4 16.3 %copy-start.94 = (f32[576]{0:T(1024)S(1)}, f32[576]{0:T(1024)}, u32[]{:S(2)}) copy-start(f32[576]{0:T(1024)} %copy-done.93) | copy-start | bytes 6916
  394.4 16.3 %copy-start.109 = (f32[128]{0:T(128)S(1)}, f32[128]{0:T(128)}, u32[]{:S(2)}) copy-start(f32[128]{0:T(128)} %copy-done.108) | copy-start | bytes 1540
  397.4 14.9 %copy-start.116 = (f32[128]{0:T(128)S(1)}, f32[128]{0:T(128)}, u32[]{:S(2)}) copy-start(f32[128]{0:T(128)} %get-tuple-element.152) | copy-start | bytes 1540
  (86 other events, 245.5 us)
